TPU v7x, 256 devices: a whole 4x4x8 slice. The times are simulated.
256 devices in a mesh: grp: 2 (over z_hi), own: 128 (over z_lo, y, x, core).
Axes of the slice: x: 4, y: 4, z: 8 (z_hi: 2, z_lo: 4; z = z_hi * 4 + z_lo), core: 2. Of those that a mesh axis runs over, the one named last changes fastest.
Arguments:
- points: bfloat16 [131072, 768], P(('grp', 'own')), may hold values from -6 to 6
- list_ids: int32 [131072], P(('grp', 'own')), may hold values from 0 to 65535, as said below
- code_ids: int32 [131072, 96], P(('grp', 'own')), may hold values from 0 to 255
- list_home: int32 [65536], replicated, may hold values from 0 to 65535, as said below
- centroids: bfloat16 [65536, 768], P('own'), may hold values from -3 to 3
- rotation: bfloat16 [768, 768], replicated, may hold values from -0.21875 to 0.21875
- codebook: bfloat16 [96, 8, 256], replicated, may hold values from -6 to 6
Outputs:
- encoded_rows: bfloat16 [262144, 768], P(('grp', 'own'))
- new_codebook: float32 [96, 8, 256], replicated
- procrustes_gram: float32 [768, 768], replicated
Inputs may be any that keep to these rules, and one draw needn't show every extreme that they name: Within the 512 rows of one device, at most 8 rows have list_home[list_ids] // 512 equal to one value; in every draw one value is reached by exactly 8 rows on every device. `list_home`: each value occurs once.
All inputs are finite; a program needn't handle non-finite values.
Results may differ from a plain program's by a relative error of at most 0.0051.
Values may be sent and summed in bfloat16 or wider, within the bound.
A program may use at most 64 MiB of HBM per device.

v0:
```python
import math

import jax
import jax.numpy as jnp
from jax import lax
from jax.sharding import PartitionSpec as P


def shards(points, list_ids, code_ids, list_home, centroids, rotation, codebook):
    owners = lax.axis_size("own")
    row_count, feat_width = points.shape
    subspaces, subdim, codewords = codebook.shape
    per_owner = centroids.shape[0]
    capacity = 2 * row_count // owners
    slot_count = owners * capacity
    storage = list_home[list_ids]
    target = storage // per_owner
    local_row = storage % per_owner
    matches = (target[:, None] == jnp.arange(owners, dtype=jnp.int32)[None, :]).astype(jnp.int32)
    position = jnp.sum(jnp.cumsum(matches, axis=0) * matches, axis=1) - 1
    placed = target * capacity + position
    send_rows = jnp.zeros((slot_count, feat_width), jnp.bfloat16).at[placed].set(points)
    send_codes = jnp.zeros((slot_count, subspaces), jnp.int32).at[placed].set(code_ids)
    send_local = jnp.full((slot_count,), -1, jnp.int32).at[placed].set(local_row)
    got_rows, got_codes, got_local = (
        lax.all_to_all(send_rows, "own", split_axis=0, concat_axis=0, tiled=True),
        lax.all_to_all(send_codes, "own", split_axis=0, concat_axis=0, tiled=True),
        lax.all_to_all(send_local, "own", split_axis=0, concat_axis=0, tiled=True),
    )
    present = got_local >= 0
    centre = centroids[jnp.maximum(got_local, 0)]
    residual = jnp.where(
        present[:, None], got_rows.astype(jnp.float32) - centre.astype(jnp.float32), 0.0
    ).astype(jnp.bfloat16)
    encoded = jnp.dot(residual, rotation, preferred_element_type=jnp.float32).astype(jnp.bfloat16)
    block_rows = 256
    block_count = slot_count // block_rows
    word_index = jnp.arange(codewords, dtype=jnp.int32)

    def accumulate(loop_step, carry):
        code_sums, code_counts, gram_sum = carry
        first_slot = loop_step * block_rows
        code_block = lax.dynamic_slice_in_dim(got_codes, first_slot, block_rows, 0)
        live_block = lax.dynamic_slice_in_dim(present, first_slot, block_rows, 0)
        resid_block = lax.dynamic_slice_in_dim(residual, first_slot, block_rows, 0)
        coded_block = lax.dynamic_slice_in_dim(encoded, first_slot, block_rows, 0).reshape(
            block_rows, subspaces, subdim
        )
        onehot = (
            (code_block[:, :, None] == word_index[None, None, :]) & live_block[:, None, None]
        ).astype(jnp.bfloat16)
        rebuilt = jnp.einsum("bmk,mjk->bmj", onehot, codebook, preferred_element_type=jnp.float32)
        rebuilt = rebuilt.astype(jnp.bfloat16).reshape(block_rows, feat_width)
        code_sums = code_sums + jnp.einsum(
            "bmk,bmj->mjk", onehot, coded_block, preferred_element_type=jnp.float32
        )
        code_counts = code_counts + jnp.sum(onehot, axis=0, dtype=jnp.float32)
        gram_sum = gram_sum + lax.dot_general(
            resid_block, rebuilt, (((0,), (0,)), ((), ())), preferred_element_type=jnp.float32
        )
        return (code_sums, code_counts, gram_sum)

    initial = (
        jnp.zeros((subspaces, subdim, codewords), jnp.float32),
        jnp.zeros((subspaces, codewords), jnp.float32),
        jnp.zeros((feat_width, feat_width), jnp.float32),
    )
    code_sums, code_counts, gram_sum = lax.fori_loop(0, block_count, accumulate, initial)
    code_sums, code_counts, gram_sum = lax.psum((code_sums, code_counts, gram_sum), ("grp", "own"))
    total_rows = row_count * lax.axis_size("grp") * owners
    procrustes_gram = gram_sum / math.sqrt(total_rows)
    new_codebook = (code_sums + codebook.astype(jnp.float32)) / (code_counts[:, None, :] + 1.0)
    return (encoded, new_codebook, procrustes_gram)


def solution(mesh):
    return jax.shard_map(
        shards,
        mesh=mesh,
        in_specs=(
            P(("grp", "own"), None),
            P(("grp", "own")),
            P(("grp", "own"), None),
            P(),
            P("own", None),
            P(),
            P(),
        ),
        out_specs=(P(("grp", "own"), None), P(), P()),
        check_vma=False,
    )
```

profile of v0, /device:TPU:1, one launch (start us, length us, event | category | flops | bytes accessed | tf_op | source)
XLA Modules:
  0.0 492.7 jit_solution(6014624772516046787)
XLA Ops:
  8.0 3.6 gather_fusion
  15.5 13.8 %all-to-all-start = ((s32[128,8,1]{1,2,0:T(1,128)}), s32[128,8,1]{1,2,0:T(1,128)S(1)}, u32[]{:S(2)}, u32[]{:S(2)}) async-start(s32[128,8,1]{1,2,0:T(1,128)} %bitcast.7), calls=%async_computation | async-start | bytes 131072 | tf_op jit(solution)/shard_map/all_to_all | solution.py:28
  32.0 7.3 %all-to-all-done = s32[128,8,1]{1,2,0:T(1,128)S(1)} async-done(((s32[128,8,1]{1,2,0:T(1,128)}), s32[128,8,1]{1,2,0:T(1,128)S(1)}, u32[]{:S(2)}, u32[]{:S(2)}) %all-to-all-start) | async-done | bytes 4128 | tf_op jit(solution)/shard_map/all_to_all | solution.py:28
  40.0 5.9 %all-to-all-start.2 = ((s32[128,8,96]{2,1,0:T(8,128)}), s32[128,8,96]{2,1,0:T(8,128)S(1)}, u32[]{:S(2)}, u32[]{:S(2)}) async-start(s32[128,8,96]{2,1,0:T(8,128)} %bitcast.10), calls=%async_computation.2 | async-start | bytes 1048576 | tf_op jit(solution)/shard_map/all_to_all | solution.py:27
  45.9 4.4 scatter_custom_fusion.1
  50.3 14.0 %all-to-all-done.2 = s32[128,8,96]{2,1,0:T(8,128)S(1)} async-done(((s32[128,8,96]{2,1,0:T(8,128)}), s32[128,8,96]{2,1,0:T(8,128)S(1)}, u32[]{:S(2)}, u32[]{:S(2)}) %all-to-all-start.2) | async-done | bytes 393248 | tf_op jit(solution)/shard_map/all_to_all | solution.py:27
  65.1 6.5 %all-to-all-start.1 = ((bf16[128,8,768]{2,1,0:T(8,128)(2,1)}), bf16[128,8,768]{2,1,0:T(8,128)(2,1)S(1)}, u32[]{:S(2)}, u32[]{:S(2)}) async-start(bf16[128,8,768]{2,1,0:T(8,128)(2,1)} %bitcast.8), calls=%async_computation.1 | async-start | bytes 3145728 | tf_op jit(solution)/shard_map/all_to_all | solution.py:26
  76.1 5.2 %gather_fusion.1 = bf16[1024,768]{1,0:T(8,128)(2,1)} fusion(bf16[512,768]{1,0:T(8,128)(2,1)S(1)} %copy-done.1, s32[1024]{0:T(1024)S(1)} %broadcast_clamp_fusion), kind=kCustom, calls=%fused_computation.1 | custom fusion | bytes 3149824 | tf_op jit(solution)/shard_map/gather | solution.py:31
  83.3 29.3 %all-to-all-done.1 = bf16[128,8,768]{2,1,0:T(8,128)(2,1)S(1)} async-done(((bf16[128,8,768]{2,1,0:T(8,128)(2,1)}), bf16[128,8,768]{2,1,0:T(8,128)(2,1)S(1)}, u32[]{:S(2)}, u32[]{:S(2)}) %all-to-all-start.1) | async-done | bytes 1572896 | tf_op jit(solution)/shard_map/all_to_all | solution.py:26
  115.9 102.0 %while.18 = (s32[]{:T(128)}, f32[96,8,256]{2,1,0:T(8,128)}, f32[96,256]{1,0:T(8,128)S(1)}, f32[768,768]{1,0:T(8,128)}, bf16[1024,768]{1,0:T(8,128)(2,1)S(1)}, /*...) while((s32[]{:T(128)}, f32[96,8,256]{2,1,0:T(8,128)}, ...), condition=%wide.region_8.9_spmd.clone, body=%wide.region_6.8_spmd.clone.sunk | while | flops 561733632 | bytes 24086052 | solution.py:68
  117.1 8.6 %convert_reduce_fusion.2 = f32[96,256]{1,0:T(8,128)S(1)} fusion(s32[256,96]{0,1:T(8,128)S(1)} %constant_dynamic-slice_fusion.4, pred[256]{0:T(512)(128)(4,1)S(1)} %dynamic_slice.43), kind=kLoop, calls=%fused_computation.7.clone.1 | loop fusion | flops 31432704 | bytes 196864 | tf_op jit(solution)/shard_map/while/body/eval_jaxpr/reduce_sum | solution.py:57
  126.0 6.0 %fusion.56 = f32[96,8,256]{2,1,0:T(8,128)} fusion(s32[256,96]{0,1:T(8,128)S(1)} %constant_dynamic-slice_fusion.4, pred[256]{0:T(512)(128)(4,1)S(1)} %dynamic_slice.43, f32[96,8,256]{2,1,0:T(8,128)} %get-tuple-element.328, bf16[256,768]{0,1:T(8,128)(2,1)S(1)} %copy.24, pred[]{:T(512)S(6)} %compare.19), kind=kOutput, calls=%fused_computation.17.clone.1 | convolution fusion | flops 113639424 | bytes 2064641 | tf_op jit(solution)/shard_map/while/body/eval_jaxpr/bmk,bmj->mjk/dot_general | solution.py:54
  132.0 8.0 %select_add_fusion.5 = f32[768,768]{1,0:T(8,128)} fusion(f32[768,768]{1,0:T(8,128)} %get-tuple-element.330, pred[]{:T(512)S(6)} %compare.19, bf16[96,8,256]{2,1,0:T(8,128)(2,1)S(1)} %copy-done.11, s32[256,96]{0,1:T(8,128)S(1)} %constant_dynamic-slice_fusion.4, pred[256]{0:T(512)(128)(4,1)S(1)} %dynamic_slice.43, ...), kind=kOutput, calls=%fused_computation.16.clone.1 | convolution fusion | flops 416612352 | bytes 5603589 | tf_op jit(solution)/shard_map/while/body/eval_jaxpr/dot_general | solution.py:58
  141.1 8.6 %convert_reduce_fusion.2 = f32[96,256]{1,0:T(8,128)S(1)} fusion(s32[256,96]{0,1:T(8,128)S(1)} %constant_dynamic-slice_fusion.4, pred[256]{0:T(512)(128)(4,1)S(1)} %dynamic_slice.43), kind=kLoop, calls=%fused_computation.7.clone.1 | loop fusion | flops 31432704 | bytes 196864 | tf_op jit(solution)/shard_map/while/body/eval_jaxpr/reduce_sum | solution.py:57
  150.0 7.2 %fusion.56 = f32[96,8,256]{2,1,0:T(8,128)} fusion(s32[256,96]{0,1:T(8,128)S(1)} %constant_dynamic-slice_fusion.4, pred[256]{0:T(512)(128)(4,1)S(1)} %dynamic_slice.43, f32[96,8,256]{2,1,0:T(8,128)} %get-tuple-element.328, bf16[256,768]{0,1:T(8,128)(2,1)S(1)} %copy.24, pred[]{:T(512)S(6)} %compare.19), kind=kOutput, calls=%fused_computation.17.clone.1 | convolution fusion | flops 113639424 | bytes 2064641 | tf_op jit(solution)/shard_map/while/body/eval_jaxpr/bmk,bmj->mjk/dot_general | solution.py:54
  157.2 8.8 %select_add_fusion.5 = f32[768,768]{1,0:T(8,128)} fusion(f32[768,768]{1,0:T(8,128)} %get-tuple-element.330, pred[]{:T(512)S(6)} %compare.19, bf16[96,8,256]{2,1,0:T(8,128)(2,1)S(1)} %copy-done.11, s32[256,96]{0,1:T(8,128)S(1)} %constant_dynamic-slice_fusion.4, pred[256]{0:T(512)(128)(4,1)S(1)} %dynamic_slice.43, ...), kind=kOutput, calls=%fused_computation.16.clone.1 | convolution fusion | flops 416612352 | bytes 5603589 | tf_op jit(solution)/shard_map/while/body/eval_jaxpr/dot_general | solution.py:58
  167.1 8.6 %convert_reduce_fusion.2 = f32[96,256]{1,0:T(8,128)S(1)} fusion(s32[256,96]{0,1:T(8,128)S(1)} %constant_dynamic-slice_fusion.4, pred[256]{0:T(512)(128)(4,1)S(1)} %dynamic_slice.43), kind=kLoop, calls=%fused_computation.7.clone.1 | loop fusion | flops 31432704 | bytes 196864 | tf_op jit(solution)/shard_map/while/body/eval_jaxpr/reduce_sum | solution.py:57
  176.0 7.2 %fusion.56 = f32[96,8,256]{2,1,0:T(8,128)} fusion(s32[256,96]{0,1:T(8,128)S(1)} %constant_dynamic-slice_fusion.4, pred[256]{0:T(512)(128)(4,1)S(1)} %dynamic_slice.43, f32[96,8,256]{2,1,0:T(8,128)} %get-tuple-element.328, bf16[256,768]{0,1:T(8,128)(2,1)S(1)} %copy.24, pred[]{:T(512)S(6)} %compare.19), kind=kOutput, calls=%fused_computation.17.clone.1 | convolution fusion | flops 113639424 | bytes 2064641 | tf_op jit(solution)/shard_map/while/body/eval_jaxpr/bmk,bmj->mjk/dot_general | solution.py:54
  183.2 8.8 %select_add_fusion.5 = f32[768,768]{1,0:T(8,128)} fusion(f32[768,768]{1,0:T(8,128)} %get-tuple-element.330, pred[]{:T(512)S(6)} %compare.19, bf16[96,8,256]{2,1,0:T(8,128)(2,1)S(1)} %copy-done.11, s32[256,96]{0,1:T(8,128)S(1)} %constant_dynamic-slice_fusion.4, pred[256]{0:T(512)(128)(4,1)S(1)} %dynamic_slice.43, ...), kind=kOutput, calls=%fused_computation.16.clone.1 | convolution fusion | flops 416612352 | bytes 5603589 | tf_op jit(solution)/shard_map/while/body/eval_jaxpr/dot_general | solution.py:58
  193.1 8.6 %convert_reduce_fusion.2 = f32[96,256]{1,0:T(8,128)S(1)} fusion(s32[256,96]{0,1:T(8,128)S(1)} %constant_dynamic-slice_fusion.4, pred[256]{0:T(512)(128)(4,1)S(1)} %dynamic_slice.43), kind=kLoop, calls=%fused_computation.7.clone.1 | loop fusion | flops 31432704 | bytes 196864 | tf_op jit(solution)/shard_map/while/body/eval_jaxpr/reduce_sum | solution.py:57
  202.0 7.2 %fusion.56 = f32[96,8,256]{2,1,0:T(8,128)} fusion(s32[256,96]{0,1:T(8,128)S(1)} %constant_dynamic-slice_fusion.4, pred[256]{0:T(512)(128)(4,1)S(1)} %dynamic_slice.43, f32[96,8,256]{2,1,0:T(8,128)} %get-tuple-element.328, bf16[256,768]{0,1:T(8,128)(2,1)S(1)} %copy.24, pred[]{:T(512)S(6)} %compare.19), kind=kOutput, calls=%fused_computation.17.clone.1 | convolution fusion | flops 113639424 | bytes 2064641 | tf_op jit(solution)/shard_map/while/body/eval_jaxpr/bmk,bmj->mjk/dot_general | solution.py:54
  209.2 8.8 %select_add_fusion.5 = f32[768,768]{1,0:T(8,128)} fusion(f32[768,768]{1,0:T(8,128)} %get-tuple-element.330, pred[]{:T(512)S(6)} %compare.19, bf16[96,8,256]{2,1,0:T(8,128)(2,1)S(1)} %copy-done.11, s32[256,96]{0,1:T(8,128)S(1)} %constant_dynamic-slice_fusion.4, pred[256]{0:T(512)(128)(4,1)S(1)} %dynamic_slice.43, ...), kind=kOutput, calls=%fused_computation.16.clone.1 | convolution fusion | flops 416612352 | bytes 5603589 | tf_op jit(solution)/shard_map/while/body/eval_jaxpr/dot_general | solution.py:58
  218.6 262.0 %all-reduce.3.cloned.1.call-done = (f32[96,8,256]{2,1,0:T(8,128)}, f32[96,256]{1,0:T(8,128)}, f32[768,768]{1,0:T(8,128)}) async-done(((f32[96,8,256]{2,1,0:T(8,128)}, f32[96,256]{1,0:T(8,128)}, f32[768,768]{1,0:T(8,128)}), (f32[96,8,256]{2,1,0:T(8,128)}, f32[96,256]{1,0:T(8,128)}, f32[768,768]{1,0:T(8,128)})) %all-reduce.3.cloned.1.call-update) | async-done | bytes 3244048 | tf_op jit(solution)/shard_map/psum | solution.py:69
  481.5 3.4 broadcast_multiply_fusion
  (102 shorter events, 26.3 us)
Async XLA Ops:
  7.2 107.3 %copy-start = (bf16[768,768]{1,0:T(8,128)(2,1)S(1)}, bf16[768,768]{1,0:T(8,128)(2,1)}, u32[]{:S(2)}) copy-start(bf16[768,768]{1,0:T(8,128)(2,1)} %param.14) | copy-start | bytes 3538948
  7.2 22.2 %copy-start.13 = (s32[512,96]{0,1:T(8,128)S(1)}, s32[512,96]{0,1:T(8,128)}, u32[]{:S(2)}) copy-start(s32[512,96]{0,1:T(8,128)} %param.11) | copy-start | bytes 589828
  15.5 23.8 %all-to-all-start = ((s32[128,8,1]{1,2,0:T(1,128)}), s32[128,8,1]{1,2,0:T(1,128)S(1)}, u32[]{:S(2)}, u32[]{:S(2)}) async-start(s32[128,8,1]{1,2,0:T(1,128)} %bitcast.7), calls=%async_computation | async-start | bytes 131072 | tf_op jit(solution)/shard_map/all_to_all | solution.py:28
  40.0 24.3 %all-to-all-start.2 = ((s32[128,8,96]{2,1,0:T(8,128)}), s32[128,8,96]{2,1,0:T(8,128)S(1)}, u32[]{:S(2)}, u32[]{:S(2)}) async-start(s32[128,8,96]{2,1,0:T(8,128)} %bitcast.10), calls=%async_computation.2 | async-start | bytes 1048576 | tf_op jit(solution)/shard_map/all_to_all | solution.py:27
  45.9 30.2 %copy-start.1 = (bf16[512,768]{1,0:T(8,128)(2,1)S(1)}, bf16[512,768]{1,0:T(8,128)(2,1)}, u32[]{:S(2)}) copy-start(bf16[512,768]{1,0:T(8,128)(2,1)} %param.13) | copy-start | bytes 2359300
  65.1 47.4 %all-to-all-start.1 = ((bf16[128,8,768]{2,1,0:T(8,128)(2,1)}), bf16[128,8,768]{2,1,0:T(8,128)(2,1)S(1)}, u32[]{:S(2)}, u32[]{:S(2)}) async-start(bf16[128,8,768]{2,1,0:T(8,128)(2,1)} %bitcast.8), calls=%async_computation.1 | async-start | bytes 3145728 | tf_op jit(solution)/shard_map/all_to_all | solution.py:26
  71.7 409.0 %all-reduce.3.cloned.1.call-start = ((), (), s32[]{:S(2)}) async-start(), calls=%async_computation.3 | async-start | bytes 6488064 | tf_op jit(solution)/shard_map/psum | solution.py:69
  76.1 36.5 %copy-start.14 = (pred[1024]{0:T(1024)(128)(4,1)S(1)}, pred[1024]{0:T(1024)(128)(4,1)}, u32[]{:S(2)}) copy-start(pred[1024]{0:T(1024)(128)(4,1)} %ge.11) | copy-start | bytes 3076
  114.5 1.4 copy-start.8
  115.9 9.8 %copy-start.4 = (bf16[1024,768]{1,0:T(8,128)(2,1)}, bf16[1024,768]{1,0:T(8,128)(2,1)S(1)}, u32[]{:S(2)}) copy-start(bf16[1024,768]{1,0:T(8,128)(2,1)S(1)} %get-tuple-element.344) | copy-start | bytes 4718596 | tf_op jit(solution)/shard_map/while
  126.0 6.0 %copy-start.11 = (bf16[96,8,256]{2,1,0:T(8,128)(2,1)S(1)}, bf16[96,8,256]{2,1,0:T(8,128)(2,1)}, u32[]{:S(2)}) copy-start(bf16[96,8,256]{2,1,0:T(8,128)(2,1)} %get-tuple-element.348) | copy-start | bytes 1179652 | tf_op jit(solution)/shard_map/while
  132.0 8.0 %copy-start.5 = (bf16[1024,768]{1,0:T(8,128)(2,1)S(1)}, bf16[1024,768]{1,0:T(8,128)(2,1)}, u32[]{:S(2)}) copy-start(bf16[1024,768]{1,0:T(8,128)(2,1)} %copy-done.4) | copy-start | bytes 4718596 | tf_op jit(solution)/shard_map/while
  140.0 9.8 %copy-start.4 = (bf16[1024,768]{1,0:T(8,128)(2,1)}, bf16[1024,768]{1,0:T(8,128)(2,1)S(1)}, u32[]{:S(2)}) copy-start(bf16[1024,768]{1,0:T(8,128)(2,1)S(1)} %get-tuple-element.344) | copy-start | bytes 4718596 | tf_op jit(solution)/shard_map/while
  150.0 7.2 %copy-start.11 = (bf16[96,8,256]{2,1,0:T(8,128)(2,1)S(1)}, bf16[96,8,256]{2,1,0:T(8,128)(2,1)}, u32[]{:S(2)}) copy-start(bf16[96,8,256]{2,1,0:T(8,128)(2,1)} %get-tuple-element.348) | copy-start | bytes 1179652 | tf_op jit(solution)/shard_map/while
  157.2 8.8 %copy-start.5 = (bf16[1024,768]{1,0:T(8,128)(2,1)S(1)}, bf16[1024,768]{1,0:T(8,128)(2,1)}, u32[]{:S(2)}) copy-start(bf16[1024,768]{1,0:T(8,128)(2,1)} %copy-done.4) | copy-start | bytes 4718596 | tf_op jit(solution)/shard_map/while
  166.0 9.8 %copy-start.4 = (bf16[1024,768]{1,0:T(8,128)(2,1)}, bf16[1024,768]{1,0:T(8,128)(2,1)S(1)}, u32[]{:S(2)}) copy-start(bf16[1024,768]{1,0:T(8,128)(2,1)S(1)} %get-tuple-element.344) | copy-start | bytes 4718596 | tf_op jit(solution)/shard_map/while
  176.0 7.2 %copy-start.11 = (bf16[96,8,256]{2,1,0:T(8,128)(2,1)S(1)}, bf16[96,8,256]{2,1,0:T(8,128)(2,1)}, u32[]{:S(2)}) copy-start(bf16[96,8,256]{2,1,0:T(8,128)(2,1)} %get-tuple-element.348) | copy-start | bytes 1179652 | tf_op jit(solution)/shard_map/while
  183.2 8.8 %copy-start.5 = (bf16[1024,768]{1,0:T(8,128)(2,1)S(1)}, bf16[1024,768]{1,0:T(8,128)(2,1)}, u32[]{:S(2)}) copy-start(bf16[1024,768]{1,0:T(8,128)(2,1)} %copy-done.4) | copy-start | bytes 4718596 | tf_op jit(solution)/shard_map/while
  192.0 9.8 %copy-start.4 = (bf16[1024,768]{1,0:T(8,128)(2,1)}, bf16[1024,768]{1,0:T(8,128)(2,1)S(1)}, u32[]{:S(2)}) copy-start(bf16[1024,768]{1,0:T(8,128)(2,1)S(1)} %get-tuple-element.344) | copy-start | bytes 4718596 | tf_op jit(solution)/shard_map/while
  202.0 7.2 %copy-start.11 = (bf16[96,8,256]{2,1,0:T(8,128)(2,1)S(1)}, bf16[96,8,256]{2,1,0:T(8,128)(2,1)}, u32[]{:S(2)}) copy-start(bf16[96,8,256]{2,1,0:T(8,128)(2,1)} %get-tuple-element.348) | copy-start | bytes 1179652 | tf_op jit(solution)/shard_map/while
  209.2 8.8 %copy-start.5 = (bf16[1024,768]{1,0:T(8,128)(2,1)S(1)}, bf16[1024,768]{1,0:T(8,128)(2,1)}, u32[]{:S(2)}) copy-start(bf16[1024,768]{1,0:T(8,128)(2,1)} %copy-done.4) | copy-start | bytes 4718596 | tf_op jit(solution)/shard_map/while
  218.0 267.9 %copy-start.6 = (bf16[1024,768]{1,0:T(8,128)(2,1)}, bf16[1024,768]{1,0:T(8,128)(2,1)S(1)}, u32[]{:S(2)}) copy-start(bf16[1024,768]{1,0:T(8,128)(2,1)S(1)} %get-tuple-element.362) | copy-start | bytes 4718596
  481.5 3.4 copy-start.9
  481.5 3.4 copy-start.12
  (4 other events, 3.5 us)
Sparse Core Ops, SparseCore 0:
  218.7 261.8 all-reduce.2
where the time goes:
time: 495 us; the launch traced here: 493 us
  waiting for transfers between devices  313 us (63%)
  matrix products  63.3 us (13%)
  other arithmetic  45.9 us (9%)
  local copies, waits for them, and re-layouts  30.2 us (6%)
  starting transfers between devices  26.3 us (5%)
  between operations  14.3 us (3%)
    psum x1, waiting for transfers between devices, shards(): lax.psum((code_sums, code_counts, gram_sum), ('grp', 'own'))  262 us
    reduce_sum x4, other arithmetic, accumulate(): code_counts = code_counts + jnp.sum(onehot, axis=0, dtype=jnp.float32)  34.5 us
    dot_general x4, matrix products, accumulate(): lax.dot_general(resid_block, rebuilt, (((0,), (0,)), ((), ())), preferred...  34.3 us
    all_to_all x1, waiting for transfers between devices, shards(): lax.all_to_all(send_rows, 'own', split_axis=0, concat_axis=0, tiled=True)  29.3 us
    dot_general x4, matrix products, accumulate(): jnp.einsum('bmk,bmj->mjk', onehot, coded_block, preferred_element_type=jn...  27.6 us
    all_to_all x1, waiting for transfers between devices, shards(): lax.all_to_all(send_codes, 'own', split_axis=0, concat_axis=0, tiled=True)  14 us
    all_to_all x1, starting transfers between devices, shards(): lax.all_to_all(send_local, 'own', split_axis=0, concat_axis=0, tiled=True)  13.8 us
  transfers between devices with their start and end apart: 4, of which 4 were waited for; matrix products, arithmetic and copies ran while one was open for 4% of the time, Pallas kernels for 0%

commit v1 on v0

v1 whole, which is shorter than its diff:
```python
import math

import jax
import jax.numpy as jnp
from jax import lax
from jax.experimental import pallas as pl
from jax.experimental.pallas import tpu as pltpu
from jax.sharding import PartitionSpec as P

MESH = pl.DeviceIdType.MESH
F32 = jnp.float32
BF16 = jnp.bfloat16
I32 = jnp.int32

NZ, NY, NX = 8, 4, 4
OWN = 128
CAP = 8
ROWS = 512
D = 768
M = 96
SLOTS = OWN * CAP
Q = 48
ROW_CHUNKS = 4


def dot(a, b, dims):
    return lax.dot_general(a, b, (dims, ((), ())), preferred_element_type=F32)


def nn(a, b):
    return dot(a, b, ((1,), (0,)))


def nt(a, b):
    return dot(a, b, ((1,), (1,)))


def tn(a, b):
    return dot(a, b, ((0,), (0,)))


def tt(a, b):
    return dot(a, b, ((0,), (1,)))


def iota(shape, axis):
    return lax.broadcasted_iota(I32, shape, axis)


def kernel(
    points, ids, code_ids, home, centroids, rotation, codebook,
    enc_out, book_out, gram_out,
    srow, rrow, scode, rcode, slot_s, pcodes, ccodes, ehi, elo, reb, crt_hi, crt_lo,
    centre, onel, local_s, gram, sums, counts,
    s0g, s0s, r0g, r0s, s1g, s1s, r1g, r1s, s2g, s2s, r2g, r2s, s3g, s3s, r3g, r3s,
    fin, a4, a5g, a5s, a6g, a6s, a7g, a7s,
    code_send, code_recv, row_send, row_recv, red_send, red_recv, sem_a, sem_b, own_sem,
):
    me = lax.axis_index("own")
    z = lax.axis_index("grp") * 4 + me // 32
    zl = me // 32
    y = (me // 8) % 4
    x = (me // 2) % 4
    c = me % 2
    other = 1 - c

    def at(z_, y_, x_, c_):
        return {"grp": z_ // 4, "own": (z_ % 4) * 32 + y_ * 8 + x_ * 2 + c_}

    line_x = [at(z, y, (x + d) % 4, (c + e) % 2) for d in range(4) for e in range(2) if d or e]
    line_y = [at(z, (y + d) % 4, x, c) for d in range(1, 4)]
    line_z = [at((z + d) % 8, y, x, c) for d in range(1, 8)]
    barrier = pltpu.get_barrier_semaphore()
    for peer in line_x + line_y + line_z:
        pl.semaphore_signal(barrier, inc=1, device_id=peer, device_id_type=MESH)

    row_id = ids[...]
    id_hi = lax.shift_right_logical(row_id, 7)
    id_lo = row_id & 127
    pick = (iota((512, ROWS), 0) == id_hi).astype(F32).astype(BF16)
    table = home[...]
    table_hi = lax.shift_right_logical(table, 8).astype(F32).astype(BF16)
    table_lo = (table & 255).astype(F32).astype(BF16)
    lane = iota((128, ROWS), 0) == id_lo
    st_hi = jnp.sum(jnp.where(lane, tn(table_hi, pick), 0.0), axis=0, keepdims=True)
    st_lo = jnp.sum(jnp.where(lane, tn(table_lo, pick), 0.0), axis=0, keepdims=True)
    storage = st_hi.astype(I32) * 256 + st_lo.astype(I32)
    owner = lax.shift_right_logical(storage, 9)
    local = storage & 511
    match = (iota((OWN, ROWS), 0) == owner).astype(F32)
    before = (iota((ROWS, ROWS), 0) < iota((ROWS, ROWS), 1)).astype(F32).astype(BF16)
    earlier = nn(match.astype(BF16), before)
    position = jnp.sum(match * earlier, axis=0, keepdims=True).astype(I32)
    slot_s[...] = owner * CAP + position

    eye = (iota((128, M), 0) == iota((128, M), 1)).astype(F32).astype(BF16)
    turned = nt(eye, code_ids[...].astype(F32).astype(BF16))
    pcodes[...] = turned.astype(I32)
    line = iota((128, ROWS), 0)
    aux = jnp.where(line == 96, (lax.shift_right_logical(local, 8)).astype(F32), 0.0)
    aux = aux + jnp.where(line == 97, (local & 255).astype(F32), 0.0)
    aux = aux + jnp.where(line == 98, 1.0, 0.0)
    packed = (turned + aux).astype(BF16)

    def place(i):
        return (iota((128, ROWS), 0) + 128 * i == slot_s[...]).astype(F32).astype(BF16)

    def codes_chunk(i, _):
        block = nt(place(i), packed)
        scode[pl.ds(16 * i, 16)] = block.reshape(16, CAP, 128).astype(BF16)
        return 0

    lax.fori_loop(0, 8, codes_chunk, 0)

    def rows_chunk(i, _):
        block = nn(place(i), points[...])
        srow[pl.ds(16 * i, 16)] = block.reshape(16, CAP, D).astype(BF16)
        return 0

    lax.fori_loop(0, 8, rows_chunk, 0)

    pl.semaphore_wait(barrier, 17)
    for peer in line_x:
        pl.semaphore_signal(sem_a, inc=1, device_id=peer, device_id_type=MESH)
    pl.semaphore_wait(sem_a, 7)
    for peer in line_y:
        pl.semaphore_signal(sem_b, inc=1, device_id=peer, device_id_type=MESH)
    pl.semaphore_wait(sem_b, 3)

    def code_copy(k):
        to = me ^ k
        return pltpu.make_async_remote_copy(
            src_ref=scode.at[to], dst_ref=rcode.at[me], send_sem=code_send, recv_sem=code_recv,
            device_id={"own": to}, device_id_type=MESH)

    def send_code(k, _):
        code_copy(k).start()
        return 0

    lax.fori_loop(1, OWN, send_code, 0)

    def row_copy(to):
        return pltpu.make_async_remote_copy(
            src_ref=srow.at[to], dst_ref=rrow.at[me], send_sem=row_send,
            recv_sem=row_recv.at[zl], device_id={"own": to}, device_id_type=MESH)

    def send_row(k, _):
        row_copy(me ^ ((k % 4) * 32 + k // 4)).start()
        return 0

    lax.fori_loop(1, OWN, send_row, 0)
    rcode[me] = scode[me]
    rrow[me] = srow[me]

    def split(value, at_, cols):
        hi = value.astype(BF16)
        ehi[at_, cols] = hi
        elo[at_, cols] = (value - hi.astype(F32)).astype(BF16)

    for i in range(3):
        rows_i = pl.ds(256 * i, 256)
        split(tt(rotation[:, 256 * i:256 * i + 256], points[...]), rows_i, pl.ds(0, ROWS))
        part = -tt(rotation[:, 256 * i:256 * i + 256], centroids[...])
        hi = part.astype(BF16)
        crt_hi[rows_i, :] = hi
        crt_lo[rows_i, :] = (part - hi.astype(F32)).astype(BF16)

    def group(g, codes, n, with_counts):
        rhs, high = [], []
        for ml in range(4):
            code = codes[pl.ds(4 * g + ml, 1), pl.ds(0, n)]
            rhs.append((iota((64, n), 0) == (code & 63)).astype(F32).astype(BF16))
            wide = jnp.broadcast_to(code, (8, n))
            book = codebook[4 * g + ml].astype(F32)
            parts = []
            for b in range(n // 128):
                idx = wide[:, 128 * b:128 * b + 128]
                low_idx = idx & 127
                first = jnp.take_along_axis(book[:, :128], low_idx, axis=1)
                second = jnp.take_along_axis(book[:, 128:], low_idx, axis=1)
                parts.append(jnp.where(idx < 128, first, second))
            high.append(lax.shift_right_arithmetic(wide, 6))
            reb_rows = jnp.concatenate(parts, axis=1)
            high[-1] = (high[-1], reb_rows)
        reb[pl.ds(pl.multiple_of(32 * g, 32), 32), pl.ds(0, n)] = jnp.concatenate(
            [h[1] for h in high], axis=0).astype(BF16)
        upper = jnp.concatenate([h[0] for h in high], axis=0)
        rhs = jnp.concatenate(rhs, axis=0)
        rows_g = pl.ds(pl.multiple_of(32 * g, 32), 32)
        e1 = ehi[rows_g, pl.ds(0, n)].astype(F32)
        e2 = elo[rows_g, pl.ds(0, n)].astype(F32)
        masks = [upper == a for a in range(4)]
        lhs = [jnp.where(k, e1, 0.0).astype(BF16) for k in masks]
        lhs += [jnp.where(k, e2, 0.0).astype(BF16) for k in masks]
        if with_counts:
            lhs += [k.astype(F32).astype(BF16) for k in masks]
        out = nt(jnp.concatenate(lhs, axis=0), rhs)
        keep = (iota((32, 256), 0) // 8) == (iota((32, 256), 1) // 64)
        left = iota((32, 128), 1) < 64

        def fold(v):
            v = jnp.where(keep, v, 0.0)
            v = v[:, :128] + v[:, 128:]
            return v + pltpu.roll(v, 64, 1)

        s = [fold(out[32 * a:32 * a + 32] + out[128 + 32 * a:160 + 32 * a]) for a in range(4)]
        s_lo, s_hi = jnp.where(left, s[0], s[1]), jnp.where(left, s[2], s[3])
        if with_counts:
            k = [fold(out[256 + 32 * a:288 + 32 * a]) for a in range(4)]
            counts[rows_g, :] = jnp.concatenate(
                [jnp.where(left, k[0], k[1]), jnp.where(left, k[2], k[3])], axis=1)
            sums[rows_g, :] = jnp.concatenate([s_lo, s_hi], axis=1)
        else:
            sums[rows_g, :] += jnp.concatenate([s_lo, s_hi], axis=1)

    def own_group(g, _):
        group(g, pcodes, ROWS, True)
        return 0

    lax.fori_loop(0, M // 4, own_group, 0)
    for i in range(3):
        cols = pl.ds(256 * i, 256)
        gram[cols, :] = tt(points[:, 256 * i:256 * i + 256], reb[:, pl.ds(0, ROWS)])

    pltpu.make_async_copy(rcode.at[pl.ds(0, OWN - 1)], rcode.at[pl.ds(0, OWN - 1)], code_recv).wait()
    ident = (iota((128, 128), 0) == iota((128, 128), 1)).astype(F32).astype(BF16)
    got = nt(ident, rcode[...].astype(F32).reshape(SLOTS, 128).astype(BF16))
    ccodes[...] = got.astype(I32)
    here = got[96:97, :] * 256.0 + got[97:98, :] - 1024.0 * (1.0 - got[98:99, :])
    local_s[...] = here.astype(I32)
    onel[...] = (iota((512, SLOTS), 0) == local_s[...]).astype(F32).astype(BF16)
    for i in range(3):
        rows_i = pl.ds(256 * i, 256)
        ehi[rows_i, :] = nn(crt_hi[rows_i, :], onel[...]).astype(BF16)
        elo[rows_i, :] = nn(crt_lo[rows_i, :], onel[...]).astype(BF16)

    def got_group(g, _):
        group(g, ccodes, SLOTS, False)
        return 0

    lax.fori_loop(0, M // 4, got_group, 0)
    for i in range(3):
        cols = pl.ds(256 * i, 256)
        turned_c = tn(centroids[:, 256 * i:256 * i + 256], onel[...]).astype(BF16)
        gram[cols, :] -= nt(turned_c, reb[...])
    for i in range(4):
        centre[pl.ds(256 * i, 256), :] = tn(onel[:, 256 * i:256 * i + 256], centroids[...]).astype(BF16)

    state = [0]
    sent = []

    def remote(src, dst, peer):
        k = state[0]
        state[0] += 1
        copy = pltpu.make_async_remote_copy(
            src_ref=src, dst_ref=dst, send_sem=red_send.at[k], recv_sem=red_recv.at[k],
            device_id=peer, device_id_type=MESH)
        copy.start()
        sent.append(copy)
        return copy

    def arrive(copies):
        for copy in copies:
            copy.wait_recv()

    s0g[...] = gram[:, pl.ds(384 * other, 384)].reshape(16, Q, 384).astype(BF16)
    s0s[:, :, 0:128] = sums[:, pl.ds(128 * other, 128)].reshape(16, Q, 128).astype(BF16)
    s0s[:, :, 128:256] = counts[:, pl.ds(128 * other, 128)].reshape(16, Q, 128).astype(BF16)
    peer_c = at(z, y, x, other)
    copies = [remote(s0g, r0g, peer_c), remote(s0s, r0s, peer_c)]
    arrive(copies)
    mine_g = gram[:, pl.ds(384 * c, 384)].reshape(16, Q, 384)
    s1g[...] = (mine_g + r0g[...].astype(F32)).astype(BF16)
    mine_s = jnp.concatenate([sums[:, pl.ds(128 * c, 128)], counts[:, pl.ds(128 * c, 128)]], axis=1)
    s1s[...] = (mine_s.reshape(16, Q, 256) + r0s[...].astype(F32)).astype(BF16)

    copies = []
    for d in range(1, 4):
        x2, y2 = (x + d) % 4, (y + d) % 4
        copies.append(remote(s1g.at[pl.ds(4 * x2, 4)], r1g.at[d - 1], at(z, y, x2, c)))
        copies.append(remote(s1s.at[pl.ds(4 * y2, 4)], r1s.at[d - 1], at(z, y2, x, c)))
    arrive(copies)
    own_g = s1g[pl.ds(4 * x, 4)].astype(F32)
    own_s = s1s[pl.ds(4 * y, 4)].astype(F32)
    for d in range(3):
        own_g = own_g + r1g[d].astype(F32)
        own_s = own_s + r1s[d].astype(F32)
    s2g[...] = own_g.astype(BF16)
    s2s[...] = own_s.astype(BF16)

    copies = []
    for d in range(1, 4):
        x2, y2 = (x + d) % 4, (y + d) % 4
        copies.append(remote(s2g.at[y2], r2g.at[d - 1], at(z, y2, x, c)))
        copies.append(remote(s2s.at[x2], r2s.at[d - 1], at(z, y, x2, c)))
    arrive(copies)
    own_g = s2g[y].astype(F32)
    own_s = s2s[x].astype(F32)
    for d in range(3):
        own_g = own_g + r2g[d].astype(F32)
        own_s = own_s + r2s[d].astype(F32)
    for p in range(6):
        s3g[p] = own_g[24 * (p // 3):24 * (p // 3) + 24, 128 * (p % 3):128 * (p % 3) + 128]
    for p in range(2):
        s3s[p] = own_s[24 * p:24 * p + 24, :]

    base = state[0]

    def z_copy(d, is_gram):
        z2 = (z + d) % 8
        k = base + d - 1
        if is_gram:
            src, dst = s3g.at[jnp.minimum(z2, 5)], r3g.at[d - 1]
        else:
            src, dst = s3s.at[jnp.maximum(z2 - 6, 0)], r3s.at[d - 1]
        return pltpu.make_async_remote_copy(
            src_ref=src, dst_ref=dst, send_sem=red_send.at[k], recv_sem=red_recv.at[k],
            device_id=at(z2, y, x, c), device_id_type=MESH)

    for d in range(1, 8):
        z2 = (z + d) % 8

        @pl.when(z2 < 6)
        def _():
            z_copy(d, True).start()

        @pl.when(z2 >= 6)
        def _():
            z_copy(d, False).start()

    state[0] += 7

    @pl.when(z < 6)
    def _():
        total = s3g[jnp.minimum(z, 5)]
        for d in range(1, 8):
            z_copy(d, True).wait_recv()
            total = total + r3g[d - 1]
        fin[...] = total * (1.0 / math.sqrt(OWN * 2 * ROWS))

    @pl.when(z >= 6)
    def _():
        part = jnp.maximum(z - 6, 0)
        total = s3s[part]
        for d in range(1, 8):
            z_copy(d, False).wait_recv()
            total = total + r3s[d - 1]
        first = 6 * (4 * y + x) + 3 * part
        old = codebook[pl.ds(first, 3), :, pl.ds(128 * c, 128)].astype(F32).reshape(24, 128)
        fin[...] = (total[:, :128] + old) / (total[:, 128:] + 1.0)

    copies = [remote(fin, a4.at[z], at((z + d) % 8, y, x, c)) for d in range(1, 8)]
    a4[z] = fin[...]
    arrive(copies)
    a5g[y] = jnp.concatenate(
        [jnp.concatenate([a4[3 * h + k] for k in range(3)], axis=1) for h in range(2)], axis=0
    ).astype(BF16)
    a5s[x] = jnp.concatenate([a4[6], a4[7]], axis=0).astype(BF16)

    copies = []
    for d in range(1, 4):
        x2, y2 = (x + d) % 4, (y + d) % 4
        copies.append(remote(a5g.at[y], a5g.at[y], at(z, y2, x, c)))
        copies.append(remote(a5s.at[x], a5s.at[x], at(z, y, x2, c)))
    arrive(copies)
    a6g[pl.ds(4 * x, 4)] = a5g[...]
    a6s[pl.ds(4 * y, 4)] = a5s[...]
    copies = []
    for d in range(1, 4):
        x2, y2 = (x + d) % 4, (y + d) % 4
        copies.append(remote(a6g.at[pl.ds(4 * x, 4)], a6g.at[pl.ds(4 * x, 4)], at(z, y, x2, c)))
        copies.append(remote(a6s.at[pl.ds(4 * y, 4)], a6s.at[pl.ds(4 * y, 4)], at(z, y2, x, c)))
    arrive(copies)
    copies = [remote(a6g, a7g, peer_c), remote(a6s, a7s, peer_c)]
    gram_out[:, pl.ds(384 * c, 384)] = a6g[...].astype(F32).reshape(D, 384)
    book_out[:, :, pl.ds(128 * c, 128)] = a6s[...].astype(F32).reshape(M, 8, 128)

    for s in range(ROW_CHUNKS):
        blocks = pl.ds(32 * s, 32)

        @pl.when(zl == s)
        def _():
            pltpu.make_async_copy(
                rrow.at[pl.ds(0, 31)], rrow.at[pl.ds(0, 31)], row_recv.at[s]).wait()

        @pl.when(zl != s)
        def _():
            pltpu.make_async_copy(rrow.at[blocks], rrow.at[blocks], row_recv.at[s]).wait()

        rows_s = rrow[blocks].astype(F32).reshape(256, D)
        resid = (rows_s - centre[pl.ds(256 * s, 256), :].astype(F32)).astype(BF16)
        enc_out[pl.ds(256 * s, 256), :] = nn(resid, rotation[...]).astype(BF16)

    arrive(copies)
    gram_out[:, pl.ds(384 * other, 384)] = a7g[...].astype(F32).reshape(D, 384)
    book_out[:, :, pl.ds(128 * other, 128)] = a7s[...].astype(F32).reshape(M, 8, 128)
    for copy in sent:
        copy.wait_send()
    for d in range(1, 8):
        z2 = (z + d) % 8

        @pl.when(z2 < 6)
        def _():
            z_copy(d, True).wait_send()

        @pl.when(z2 >= 6)
        def _():
            z_copy(d, False).wait_send()

    pltpu.make_async_copy(scode.at[pl.ds(0, OWN - 1)], scode.at[pl.ds(0, OWN - 1)], code_send).wait()
    pltpu.make_async_copy(srow.at[pl.ds(0, OWN - 1)], srow.at[pl.ds(0, OWN - 1)], row_send).wait()


def shards(points, list_ids, code_ids, list_home, centroids, rotation, codebook):
    vmem = pl.BlockSpec(memory_space=pltpu.VMEM)
    scratch = [
        ((OWN, CAP, D), BF16), ((OWN, CAP, D), BF16), ((OWN, CAP, 128), BF16), ((OWN, CAP, 128), BF16),
        ((1, ROWS), I32), ((128, ROWS), I32), ((128, SLOTS), I32),
        ((D, SLOTS), BF16), ((D, SLOTS), BF16), ((D, SLOTS), BF16), ((D, 512), BF16), ((D, 512), BF16),
        ((SLOTS, D), BF16), ((512, SLOTS), BF16), ((1, SLOTS), I32),
        ((D, D), F32), ((D, 256), F32), ((D, 256), F32),
        ((16, Q, 384), BF16), ((16, Q, 256), BF16), ((16, Q, 384), BF16), ((16, Q, 256), BF16),
        ((16, Q, 384), BF16), ((16, Q, 256), BF16), ((3, 4, Q, 384), BF16), ((3, 4, Q, 256), BF16),
        ((4, Q, 384), BF16), ((4, Q, 256), BF16), ((3, Q, 384), BF16), ((3, Q, 256), BF16),
        ((6, 24, 128), F32), ((2, 24, 256), F32), ((7, 24, 128), F32), ((7, 24, 256), F32),
        ((24, 128), F32), ((8, 24, 128), F32), ((4, Q, 384), BF16), ((4, Q, 128), BF16),
        ((16, Q, 384), BF16), ((16, Q, 128), BF16), ((16, Q, 384), BF16), ((16, Q, 128), BF16),
    ]
    dma = pltpu.SemaphoreType.DMA
    encoded, book, gram = pl.pallas_call(
        kernel,
        out_shape=(
            jax.ShapeDtypeStruct((SLOTS, D), BF16),
            jax.ShapeDtypeStruct((M, 8, 256), F32),
            jax.ShapeDtypeStruct((D, D), F32),
        ),
        in_specs=[vmem] * 7,
        out_specs=(vmem, vmem, vmem),
        scratch_shapes=[pltpu.VMEM(s, t) for s, t in scratch] + [
            dma, dma, dma, dma((ROW_CHUNKS,)), dma((42,)), dma((42,)),
            pltpu.SemaphoreType.REGULAR, pltpu.SemaphoreType.REGULAR, dma,
        ],
        compiler_params=pltpu.CompilerParams(
            collective_id=0, has_side_effects=True, vmem_limit_bytes=60 * 2**20),
    )(
        points, list_ids.reshape(1, ROWS), code_ids, list_home.reshape(512, 128),
        centroids, rotation, codebook,
    )
    return encoded, book, gram


def solution(mesh):
    return jax.shard_map(
        shards,
        mesh=mesh,
        in_specs=(
            P(("grp", "own"), None),
            P(("grp", "own")),
            P(("grp", "own"), None),
            P(),
            P("own", None),
            P(),
            P(),
        ),
        out_specs=(P(("grp", "own"), None), P(), P()),
        check_vma=False,
    )
```

time: 495 us -> 101 us (0.20)
  waiting for transfers between devices: 313 us -> 0 us
  Pallas kernels: 0 us -> 93.1 us
  matrix products: 63.3 us -> 0 us
  other arithmetic: 45.9 us -> 0 us
  starting transfers between devices: 26.3 us -> 0 us
  local copies, waits for them, and re-layouts: 30.2 us -> 6.86 us
  between operations: 14.3 us -> 0.66 us
    psum x1 -> x0, waiting for transfers between devices: 262 us -> none  [shards(): lax.psum((code_sums, code_counts, gram_sum), ('grp', 'own'))]
    pallas_call x0 -> x1, Pallas kernels: none -> 93.1 us  [shards(): pl.pallas_call(kernel, out_shape=(jax.ShapeDtypeStruct((SLOTS, D), BF16),...]
    dot_general x9 -> x0, matrix products: 63.3 us -> none  [the longest x4 34.3 us: accumulate(): lax.dot_general(resid_block, rebuilt, (((0,), (0,)), ((), ())), preferred...]
    all_to_all x3 -> x0, waiting for transfers between devices: 50.6 us -> none  [the longest x1 29.3 us: shards(): lax.all_to_all(send_rows, 'own', split_axis=0, concat_axis=0, tiled=True)]
    reduce_sum x5 -> x0, other arithmetic: 34.8 us -> none  [the longest x4 34.5 us: accumulate(): code_counts = code_counts + jnp.sum(onehot, axis=0, dtype=jnp.float32)]
    all_to_all x3 -> x0, starting transfers between devices: 26.3 us -> none  [the longest x1 13.8 us: shards(): lax.all_to_all(send_local, 'own', split_axis=0, concat_axis=0, tiled=True)]
    scatter x3 -> x0, local copies, waits for them, and re-layouts: 9.35 us -> none  [the longest x1 4.42 us: shards(): jnp.zeros((slot_count, feat_width), jnp.bfloat16).at[placed].set(points)]
    gather x2 -> x0, local copies, waits for them, and re-layouts: 8.85 us -> none  [the longest x1 5.21 us: shards(): centre = centroids[jnp.maximum(got_local, 0)]]
  transfers between devices with their start and end apart: 4 -> 0, of which waited for: 4 -> 0; matrix products, arithmetic and copies ran while one was open for 4% -> 0% of each run, Pallas kernels for 0% -> 0%
where the time goes in v1:
time: 101 us
  Pallas kernels  93.1 us (92%)
  local copies, waits for them, and re-layouts  6.86 us (7%)
    pallas_call x1, Pallas kernels, shards(): pl.pallas_call(kernel, out_shape=(jax.ShapeDtypeStruct((SLOTS, D), BF16),...  93.1 us
    unnamed x8, local copies, waits for them, and re-layouts  6.86 us

profile of v1, /device:TPU:1, one launch (start us, length us, event | category | flops | bytes accessed | tf_op | source)
XLA Modules:
  0.0 100.6 jit_solution(3720201938039809414)
XLA Ops:
  0.6 1.8 %copy.10.code_ids = s32[512,96]{1,0:T(8,128)} copy(s32[512,96]{0,1:T(8,128)} %param.9) | data formatting | bytes 393216 | tf_op args[2]
  2.4 93.1 %shard_map.94 = (bf16[1024,768]{1,0:T(8,128)(2,1)}, f32[96,8,256]{2,1,0:T(8,128)}, f32[768,768]{1,0:T(8,128)}) custom-call(bf16[512,768]{1,0:T(8,128)(2,1)} %points.1, s32[1,512]{1,0:T(1,128)} %bitcast.3, s32[512,96]{1,0:T(8,128)} %copy.10.code_ids, s32[512,128]{1,0:T(8,128)} %bitcast.2, bf16[512,768]{1,0:T(8,128)(2,1)} %centroids.1, ...), custom_call_target="tpu_custom_call" | custom-call | tf_op jit(solution)/shard_map/pallas_call | solution.py:430
  95.5 0.0 copy-start.1
  95.5 0.0 copy-start
  95.5 2.8 %copy.14 = bf16[1024,768]{1,0:T(8,128)(2,1)} copy(bf16[1024,768]{1,0:T(8,128)(2,1)} %get-tuple-element.6) | data formatting | bytes 3145728
  98.3 0.0 copy-done.1
  98.3 0.9 copy.15
  99.2 0.0 copy-done
  99.2 1.4 %copy.16 = f32[768,768]{1,0:T(8,128)} copy(f32[768,768]{1,0:T(8,128)S(1)} %copy-done) | data formatting | bytes 4718592
Async XLA Ops:
  95.5 2.8 %copy-start.1 = (f32[96,8,256]{2,1,0:T(8,128)S(1)}, f32[96,8,256]{2,1,0:T(8,128)}, u32[]{:S(2)}) copy-start(f32[96,8,256]{2,1,0:T(8,128)} %get-tuple-element.7) | copy-start | bytes 2359300
  95.5 3.7 %copy-start = (f32[768,768]{1,0:T(8,128)S(1)}, f32[768,768]{1,0:T(8,128)}, u32[]{:S(2)}) copy-start(f32[768,768]{1,0:T(8,128)} %get-tuple-element.8) | copy-start | bytes 7077892

commit v2 on v1

v2 whole, which is shorter than its diff:
```python
import math

import jax
import jax.numpy as jnp
from jax import lax
from jax.experimental import pallas as pl
from jax.experimental.pallas import tpu as pltpu
from jax.sharding import PartitionSpec as P

MESH = pl.DeviceIdType.MESH
F32 = jnp.float32
BF16 = jnp.bfloat16
I32 = jnp.int32

NZ, NY, NX = 8, 4, 4
OWN = 128
CAP = 8
ROWS = 512
D = 768
M = 96
SLOTS = OWN * CAP
Q = 48
ROW_CHUNKS = 4
UNROLL = 8
CHAINS = 4


def dot(a, b, dims):
    return lax.dot_general(a, b, (dims, ((), ())), preferred_element_type=F32)


def nn(a, b):
    return dot(a, b, ((1,), (0,)))


def nt(a, b):
    return dot(a, b, ((1,), (1,)))


def tn(a, b):
    return dot(a, b, ((0,), (0,)))


def tt(a, b):
    return dot(a, b, ((0,), (1,)))


def iota(shape, axis):
    return lax.broadcasted_iota(I32, shape, axis)


def kernel(
    points_h, ids_h, codes_h, home_h, centroids_h, rotation_h, codebook_h,
    resid_h, tiles_h,
    pc, ids, code_ids, home, rotation, codebook, rot_t, where_s, resid,
    srow, rrow, scode, rcode, slot_s, ccodes, ehi, elo, reb, crt_hi, crt_lo,
    centre, onel, local_s, gram, sums, counts,
    turned_c, g0s, g0r, g1s, g1r, c0s, c0r, c1s, c1r, gzs, gzr, czs, czr, a4, a6, a7,
    code_send, code_recv, row_send, row_recv, red_send, red_recv, z_send, z_recv, a_send, a_recv, sem_a, sem_b, load_sem, out_sem,
):
    points, centroids = pc.at[pl.ds(0, ROWS)], pc.at[pl.ds(ROWS, ROWS)]
    loads = [
        pltpu.make_async_copy(src, dst, load_sem.at[k])
        for k, (src, dst) in enumerate((
            (ids_h, ids), (home_h, home), (codes_h, code_ids), (points_h, points),
            (rotation_h, rotation), (centroids_h, centroids), (codebook_h, codebook)))
    ]
    for load in loads:
        load.start()
    me = lax.axis_index("own")
    z = lax.axis_index("grp") * 4 + me // 32
    zl = me // 32
    y = (me // 8) % 4
    x = (me // 2) % 4
    c = me % 2
    other = 1 - c

    def at(z_, y_, x_, c_):
        return {"grp": z_ // 4, "own": (z_ % 4) * 32 + y_ * 8 + x_ * 2 + c_}

    line_x = [at(z, y, (x + d) % 4, (c + e) % 2) for d in range(4) for e in range(2) if d or e]
    line_y = [at(z, (y + d) % 4, x, c) for d in range(1, 4)]
    line_z = [at((z + d) % 8, y, x, c) for d in range(1, 8)]
    barrier = pltpu.get_barrier_semaphore()
    for peer in line_x + line_y + line_z:
        pl.semaphore_signal(barrier, inc=1, device_id=peer, device_id_type=MESH)

    loads[0].wait()
    loads[1].wait()
    row_id = ids[...]
    id_hi = lax.shift_right_logical(row_id, 7)
    id_lo = row_id & 127
    pick = (iota((512, ROWS), 0) == id_hi).astype(F32).astype(BF16)
    table = home[...]
    table_hi = lax.shift_right_logical(table, 8).astype(F32).astype(BF16)
    table_lo = (table & 255).astype(F32).astype(BF16)
    lane = iota((128, ROWS), 0) == id_lo
    st_hi = jnp.sum(jnp.where(lane, tn(table_hi, pick), 0.0), axis=0, keepdims=True)
    st_lo = jnp.sum(jnp.where(lane, tn(table_lo, pick), 0.0), axis=0, keepdims=True)
    storage = st_hi.astype(I32) * 256 + st_lo.astype(I32)
    owner = lax.shift_right_logical(storage, 9)
    local = storage & 511
    match = (iota((OWN, ROWS), 0) == owner).astype(F32)
    before = (iota((ROWS, ROWS), 0) < iota((ROWS, ROWS), 1)).astype(F32).astype(BF16)
    earlier = nn(match.astype(BF16), before)
    position = jnp.sum(match * earlier, axis=0, keepdims=True).astype(I32)
    slot_s[...] = owner * CAP + position

    loads[2].wait()
    pl.semaphore_wait(barrier, 17)
    for peer in line_x:
        pl.semaphore_signal(sem_a, inc=1, device_id=peer, device_id_type=MESH)
    line = iota((32, ROWS), 0)
    aux = jnp.where(line == 0, (lax.shift_right_logical(local, 8)).astype(F32), 0.0)
    aux = aux + jnp.where(line == 1, (local & 255).astype(F32), 0.0)
    aux = aux + jnp.where(line == 2, 1.0, 0.0)
    packed = jnp.concatenate([code_ids[...].astype(F32), aux], axis=0).astype(BF16)

    def code_copy(to):
        return pltpu.make_async_remote_copy(
            src_ref=scode.at[to], dst_ref=rcode.at[me], send_sem=code_send, recv_sem=code_recv,
            device_id={"own": to}, device_id_type=MESH)

    def row_copy(to):
        return pltpu.make_async_remote_copy(
            src_ref=srow.at[to], dst_ref=rrow.at[me], send_sem=row_send,
            recv_sem=row_recv.at[zl], device_id={"own": to}, device_id_type=MESH)

    order = (4, 6, 2, 5, 7, 3, 1, 0)
    for i in order:
        j = (me // 16) ^ i
        there = (iota((128, ROWS), 0) + 128 * j == slot_s[...]).astype(F32).astype(BF16)
        where_s[pl.ds(pl.multiple_of(128 * j, 128), 128), :] = there
        scode[pl.ds(16 * j, 16)] = nt(there, packed).reshape(16, CAP, 128).astype(BF16)
    pl.semaphore_wait(sem_a, 7)
    for peer in line_y:
        pl.semaphore_signal(sem_b, inc=1, device_id=peer, device_id_type=MESH)
    loads[4].wait()
    rot_t[...] = rotation[...].T
    pl.semaphore_wait(sem_b, 3)
    for i in order:
        for k in range(16):
            if i or k:
                code_copy(me ^ (16 * i + k)).start()
    loads[3].wait()
    for i in order:
        j = (me // 16) ^ i
        block = nn(where_s[pl.ds(pl.multiple_of(128 * j, 128), 128), :], points[...])
        srow[pl.ds(16 * j, 16)] = block.reshape(16, CAP, D).astype(BF16)

    def send_rows(first, last):
        for k in range(first, last):
            row_copy(me ^ ((k % 4) * 32 + k // 4)).start()

    send_rows(1, OWN)
    rcode[me] = scode[me]
    rrow[me] = srow[me]

    def split(value, at_, cols):
        hi = value.astype(BF16)
        ehi[at_, cols] = hi
        elo[at_, cols] = (value - hi.astype(F32)).astype(BF16)

    loads[5].wait()
    loads[6].wait()
    for i in range(3):
        rows_i = pl.ds(256 * i, 256)
        both = nt(rot_t[rows_i, :], pc[...])
        split(both[:, :ROWS], rows_i, pl.ds(0, ROWS))
        part = -both[:, ROWS:]
        hi = part.astype(BF16)
        crt_hi[rows_i, :] = hi
        crt_lo[rows_i, :] = (part - hi.astype(F32)).astype(BF16)

    def rebuild(g, codes, n):
        rebuilt = []
        for ml in range(4):
            wide = jnp.broadcast_to(codes[pl.ds(4 * g + ml, 1), pl.ds(0, n)], (8, n))
            book = codebook[4 * g + ml].astype(F32)
            parts = []
            for b in range(n // 128):
                idx = wide[:, 128 * b:128 * b + 128]
                low_idx = idx & 127
                first = jnp.take_along_axis(book[:, :128], low_idx, axis=1)
                second = jnp.take_along_axis(book[:, 128:], low_idx, axis=1)
                parts.append(jnp.where(idx < 128, first, second))
            rebuilt.append(jnp.concatenate(parts, axis=1))
        rows_g = pl.ds(pl.multiple_of(32 * g, 32), 32)
        reb[rows_g, pl.ds(0, n)] = jnp.concatenate(rebuilt, axis=0).astype(BF16)

    def group(g, codes, n, with_counts):
        rows_g = pl.ds(pl.multiple_of(32 * g, 32), 32)
        rhs, high = [], []
        steps = iota((16, n), 0).astype(F32).astype(BF16)
        one, zero = jnp.ones((16, n), BF16), jnp.zeros((16, n), BF16)
        for ml in range(4):
            wide = jnp.broadcast_to(codes[pl.ds(4 * g + ml, 1), pl.ds(0, n)], (8, n))
            low = (jnp.concatenate([wide, wide], axis=0) & 63).astype(F32).astype(BF16)
            rhs += [jnp.where(low == steps + jnp.asarray(16 * k, BF16), one, zero) for k in range(4)]
            high.append(lax.shift_right_arithmetic(wide, 6).astype(F32))
        upper = jnp.concatenate(high, axis=0).astype(BF16)
        e1, e2 = ehi[rows_g, pl.ds(0, n)], elo[rows_g, pl.ds(0, n)]
        none = jnp.zeros((32, n), BF16)
        masks = [upper == jnp.asarray(a, BF16) for a in range(4)]
        lhs = [jnp.where(k, e1, none) for k in masks] + [jnp.where(k, e2, none) for k in masks]
        if with_counts:
            rows_8 = pl.ds(pl.multiple_of(8 * (g // 2), 8), 8)
            of_8 = lax.shift_right_arithmetic(codes[rows_8, pl.ds(0, n)], 6)
            lhs.append(jnp.concatenate(
                [(of_8 == a).astype(F32) for a in range(4)], axis=0).astype(BF16))
        out = nt(jnp.concatenate(lhs, axis=0), jnp.concatenate(rhs, axis=0))
        left32, left8 = iota((32, 128), 1) < 64, iota((8, 128), 1) < 64

        def fold(v, keep):
            v = jnp.where(keep, v, 0.0)
            v = v[:, :128] + v[:, 128:]
            return v + pltpu.roll(v, 64, 1)

        keep = (iota((32, 256), 0) // 8) == (iota((32, 256), 1) // 64)
        s = [fold(out[32 * a:32 * a + 32] + out[128 + 32 * a:160 + 32 * a], keep) for a in range(4)]
        s = jnp.concatenate(
            [jnp.where(left32, s[0], s[1]), jnp.where(left32, s[2], s[3])], axis=1)
        if with_counts:
            sums[rows_g, :] = s
            keep = iota((8, 256), 0) == 4 * (g % 2) + iota((8, 256), 1) // 64
            k = [fold(out[256 + 8 * a:264 + 8 * a], keep) for a in range(4)]
            counts[rows_8, :] += jnp.concatenate(
                [jnp.where(left8, k[0], k[1]), jnp.where(left8, k[2], k[3])], axis=1)
        else:
            sums[rows_g, :] += s

    counts[...] = jnp.zeros_like(counts)

    def own_group(g, _):
        rebuild(g, code_ids, ROWS)
        group(g, code_ids, ROWS, True)
        return 0

    lax.fori_loop(0, M // 4, own_group, 0, unroll=UNROLL)
    for i in range(3):
        cols = pl.ds(256 * i, 256)
        gram[cols, :] = tt(points[:, 256 * i:256 * i + 256], reb[:, pl.ds(0, ROWS)])

    pltpu.make_async_copy(rcode.at[pl.ds(0, OWN - 1)], rcode.at[pl.ds(0, OWN - 1)], code_recv).wait()
    ident = (iota((128, 128), 0) == iota((128, 128), 1)).astype(F32).astype(BF16)
    got = nt(ident, rcode[...].astype(F32).reshape(SLOTS, 128).astype(BF16))
    ccodes[...] = got.astype(I32)
    here = got[96:97, :] * 256.0 + got[97:98, :] - 1024.0 * (1.0 - got[98:99, :])
    local_s[...] = here.astype(I32)
    onel[...] = (iota((512, SLOTS), 0) == local_s[...]).astype(F32).astype(BF16)

    for i in range(3):
        rows_i = pl.ds(256 * i, 256)
        turned_c[rows_i, :] = tn(centroids[:, 256 * i:256 * i + 256], onel[...]).astype(BF16)

    state = [0]
    sent = []
    q = 4 * x + y
    peer_c = at(z, y, x, other)

    def remote(src, dst, peer):
        k = state[0]
        state[0] += 1
        copy = pltpu.make_async_remote_copy(
            src_ref=src, dst_ref=dst, send_sem=red_send.at[k], recv_sem=red_recv.at[k],
            device_id=peer, device_id_type=MESH)
        copy.start()
        sent.append(copy)
        return copy

    def arrive(copies):
        for copy in copies:
            copy.wait_recv()

    def in_plane(d):
        q2 = q ^ d
        return q2, at(z, q2 % 4, q2 // 4, c)

    def counted(value):
        top = value.astype(BF16).astype(F32)
        return jnp.concatenate([top, value - top], axis=-2)

    def tiles(j, half):
        if j < 3:
            return gram[:, pl.ds(128 * (2 * j + half), 128)].reshape(16, 3, 16, 128)
        cols = pl.ds(128 * half, 128)
        rows_8 = jnp.stack([counts[6 * b:6 * b + 8, cols] for b in range(16)])
        return jnp.concatenate(
            [sums[:, cols].reshape(16, 3, 16, 128), counted(rows_8)[:, None]], axis=1)

    def settle(j, value):
        if j < 3:
            return value.astype(BF16)
        both = value[..., 3, :8, :] + value[..., 3, 8:, :]
        return jnp.concatenate(
            [value[..., :3, :, :], counted(both)[..., None, :, :]], axis=-3).astype(BF16)

    core_s = [g0s.at[0], g0s.at[1], g0s.at[2], c0s]
    core_r = [g0r.at[0], g0r.at[1], g0r.at[2], c0r]
    plane_s = [g1s.at[0], g1s.at[1], g1s.at[2], c1s]
    plane_r = [g1r.at[0], g1r.at[1], g1r.at[2], c1r]
    line_s = [gzs.at[0], gzs.at[1], gzs.at[2], czs]
    line_r = [gzr.at[0], gzr.at[1], gzr.at[2], czr]
    flight = {}

    def owner_z(j, r):
        return (3 * j + r) % 8

    def z_copy(j, r):
        to = owner_z(j, r)
        slot = jnp.maximum((z ^ to) - 1, 0)
        return pltpu.make_async_remote_copy(
            src_ref=line_s[j].at[r], dst_ref=line_r[j].at[slot], send_sem=z_send.at[j, r],
            recv_sem=z_recv.at[j, slot], device_id=at(jnp.int32(to), y, x, c), device_id_type=MESH)

    def z_arrival(j, r, d):
        return pltpu.make_async_remote_copy(
            src_ref=line_s[j].at[r], dst_ref=line_r[j].at[d - 1], send_sem=z_send.at[j, r],
            recv_sem=z_recv.at[j, d - 1], device_id=at(z ^ d, y, x, c), device_id_type=MESH)

    def back_copy(j, r, d):
        return pltpu.make_async_remote_copy(
            src_ref=a4.at[j, r], dst_ref=a4.at[j, r], send_sem=a_send.at[j, d - 1],
            recv_sem=a_recv.at[j, r], device_id=at(z ^ d, y, x, c), device_id_type=MESH)

    def to_core(j):
        core_s[j][...] = tiles(j, other).astype(BF16)
        flight["core", j] = [remote(core_s[j], core_r[j], peer_c)]

    def to_plane(j):
        arrive(flight["core", j])
        plane_s[j][...] = settle(j, tiles(j, c) + core_r[j][...].astype(F32))
        flight["plane", j] = []
        for d in range(1, 16):
            q2, peer = in_plane(d)
            flight["plane", j].append(remote(plane_s[j].at[q2], plane_r[j].at[d - 1], peer))

    def to_line(j):
        arrive(flight["plane", j])
        value = plane_s[j][q].astype(F32)
        for d in range(15):
            value = value + plane_r[j][d].astype(F32)
        value = settle(j, value)
        for r in range(3):
            line_s[j][r, 0] = value[r]
            if j == 3:
                line_s[j][r, 1] = value[3]

            @pl.when(z != owner_z(j, r))
            def _():
                z_copy(j, r).start()

    def finish_line(j):
        for r in range(3):
            @pl.when(z == owner_z(j, r))
            def _():
                total = line_s[j][r].astype(F32)
                for d in range(1, 8):
                    z_arrival(j, r, d).wait_recv()
                    total = total + line_r[j][d - 1].astype(F32)
                if j < 3:
                    a4[j, r] = (total[0] * (1.0 / math.sqrt(OWN * 2 * ROWS))).astype(BF16)
                else:
                    count = total[1, :8] + total[1, 8:]
                    count = jnp.concatenate([
                        jnp.broadcast_to(count[2 * r + k:2 * r + k + 1], (8, 128))
                        for k in range(2)], axis=0)
                    old = codebook[pl.ds(6 * q + 2 * r, 2), :, pl.ds(128 * c, 128)]
                    old = old.astype(F32).reshape(16, 128)
                    a4[j, r] = ((total[0] + old) / (count + 1.0)).astype(BF16)
                for d in range(1, 8):
                    back_copy(j, r, d).start()

    def back_plane(j):
        for r in range(3):
            @pl.when(z != owner_z(j, r))
            def _():
                back_copy(j, r, 1).wait_recv()
        a6[j, q] = a4[j]
        flight["back", j] = []
        for d in range(1, 16):
            q2, peer = in_plane(d)
            flight["back", j].append(remote(a6.at[j, q], a6.at[j, q], peer))

    outs = []

    def write(src, dst):
        out = pltpu.make_async_copy(src, dst, out_sem.at[len(outs)])
        out.start()
        outs.append(out)

    def back_core(j):
        arrive(flight["back", j])
        flight["last", j] = [remote(a6.at[j], a7.at[j], peer_c)]
        write(a6.at[j], tiles_h.at[c, j])

    def done(j):
        arrive(flight["last", j])
        write(a7.at[j], tiles_h.at[other, j])

    def got_groups(first, last):
        def got_group(g, _):
            group(g, ccodes, SLOTS, False)
            return 0

        lax.fori_loop(first, last, got_group, 0, unroll=UNROLL)

    def got_rebuild(g, _):
        rebuild(g, ccodes, SLOTS)
        return 0

    for j in range(3):
        lax.fori_loop(8 * j, 8 * j + 8, got_rebuild, 0, unroll=UNROLL)
        cols = pl.ds(256 * j, 256)
        gram[:, cols] -= nt(turned_c[...], reb[cols, :])
        to_core(j)
        if j:
            to_plane(j - 1)
    for i in range(3):
        rows_i = pl.ds(256 * i, 256)
        ehi[rows_i, :] = nn(crt_hi[rows_i, :], onel[...]).astype(BF16)
        elo[rows_i, :] = nn(crt_lo[rows_i, :], onel[...]).astype(BF16)
    to_plane(2)
    got_groups(0, 8)
    got_groups(8, 16)
    to_line(0)
    got_groups(16, 24)
    to_core(3)
    to_line(1)
    for i in range(4):
        centre[pl.ds(256 * i, 256), :] = tn(onel[:, 256 * i:256 * i + 256], centroids[...]).astype(BF16)
    to_plane(3)
    finish_line(0)
    to_line(2)
    finish_line(1)
    back_plane(0)
    finish_line(2)
    back_plane(1)
    to_line(3)
    back_plane(2)
    finish_line(3)
    back_core(0)
    back_core(1)
    back_plane(3)
    back_core(2)
    done(0)
    done(1)
    back_core(3)

    for s in range(ROW_CHUNKS):
        blocks = pl.ds(32 * s, 32)

        @pl.when(zl == s)
        def _():
            pltpu.make_async_copy(
                rrow.at[pl.ds(0, 31)], rrow.at[pl.ds(0, 31)], row_recv.at[s]).wait()

        @pl.when(zl != s)
        def _():
            pltpu.make_async_copy(rrow.at[blocks], rrow.at[blocks], row_recv.at[s]).wait()

        rows_s = rrow[blocks].astype(F32).reshape(256, D)
        part = pl.ds(256 * s, 256)
        resid[part, :] = (rows_s - centre[part, :].astype(F32)).astype(BF16)
        write(resid.at[part], resid_h.at[part])

    done(2)
    done(3)
    for out in outs:
        out.wait()
    for copy in sent:
        copy.wait_send()
    for j in range(CHAINS):
        for r in range(3):
            @pl.when(z != owner_z(j, r))
            def _():
                z_copy(j, r).wait_send()

            @pl.when(z == owner_z(j, r))
            def _():
                for d in range(1, 8):
                    back_copy(j, r, d).wait_send()
    pltpu.make_async_copy(scode.at[pl.ds(0, OWN - 1)], scode.at[pl.ds(0, OWN - 1)], code_send).wait()
    pltpu.make_async_copy(srow.at[pl.ds(0, OWN - 1)], srow.at[pl.ds(0, OWN - 1)], row_send).wait()


def finish(resid, rotation, tiles, enc_out, gram_out, book_out):
    enc_out[...] = nn(resid[...], rotation[...]).astype(BF16)
    for h in range(2):
        for b in range(tiles.shape[2]):
            for r in range(3):
                rows_r = slice(Q * b + 16 * r, Q * b + 16 * r + 16)
                for j in range(3):
                    first = 128 * (2 * j + h)
                    gram_out[rows_r, first:first + 128] = tiles[h, j, b, r].astype(F32)
                book_out[rows_r, 128 * h:128 * h + 128] = tiles[h, 3, b, r].astype(F32)


def shards(points, list_ids, code_ids, list_home, centroids, rotation, codebook):
    hbm = pl.BlockSpec(memory_space=pl.ANY)
    scratch = [
        ((2 * ROWS, D), BF16), ((1, ROWS), I32), ((M, ROWS), I32), ((512, 128), I32), ((D, D), BF16),
        ((M, 8, 256), BF16), ((D, D), BF16), ((SLOTS, ROWS), BF16), ((SLOTS, D), BF16),
        ((OWN, CAP, D), BF16), ((OWN, CAP, D), BF16), ((OWN, CAP, 128), BF16), ((OWN, CAP, 128), BF16),
        ((1, ROWS), I32), ((128, SLOTS), I32),
        ((D, SLOTS), BF16), ((D, SLOTS), BF16), ((D, SLOTS), BF16), ((D, 512), BF16), ((D, 512), BF16),
        ((SLOTS, D), BF16), ((512, SLOTS), BF16), ((1, SLOTS), I32),
        ((D, D), F32), ((D, 256), F32), ((M + 8, 256), F32),
        ((D, SLOTS), BF16),
        ((3, 16, 3, 16, 128), BF16), ((3, 16, 3, 16, 128), BF16),
        ((3, 16, 3, 16, 128), BF16), ((3, 15, 3, 16, 128), BF16),
        ((16, 4, 16, 128), BF16), ((16, 4, 16, 128), BF16),
        ((16, 4, 16, 128), BF16), ((15, 4, 16, 128), BF16),
        ((3, 3, 1, 16, 128), BF16), ((3, 7, 1, 16, 128), BF16),
        ((3, 2, 16, 128), BF16), ((7, 2, 16, 128), BF16),
        ((4, 3, 16, 128), BF16), ((4, 16, 3, 16, 128), BF16), ((4, 16, 3, 16, 128), BF16),
    ]
    dma = pltpu.SemaphoreType.DMA
    resid, tiles = pl.pallas_call(
        kernel,
        out_shape=(
            jax.ShapeDtypeStruct((SLOTS, D), BF16),
            jax.ShapeDtypeStruct((2, CHAINS, 16, 3, 16, 128), BF16),
        ),
        in_specs=[hbm] * 7,
        out_specs=(hbm,) * 2,
        scratch_shapes=[pltpu.VMEM(s, t) for s, t in scratch] + [
            dma, dma, dma, dma((ROW_CHUNKS,)), dma((128,)), dma((128,)),
            dma((4, 3)), dma((4, 7)), dma((4, 7)), dma((4, 3)),
            pltpu.SemaphoreType.REGULAR, pltpu.SemaphoreType.REGULAR, dma((7,)), dma((12,)),
        ],
        compiler_params=pltpu.CompilerParams(
            collective_id=0, has_side_effects=True, vmem_limit_bytes=60 * 2**20),
    )(
        points, list_ids.reshape(1, ROWS), code_ids.T, list_home.reshape(512, 128),
        centroids, rotation, codebook,
    )
    steps = 4
    encoded, gram, book = pl.pallas_call(
        finish,
        grid=(steps,),
        out_shape=(
            jax.ShapeDtypeStruct((SLOTS, D), BF16),
            jax.ShapeDtypeStruct((D, D), F32),
            jax.ShapeDtypeStruct((D, 256), F32),
        ),
        in_specs=[
            pl.BlockSpec((SLOTS // steps, D), lambda i: (i, 0)),
            pl.BlockSpec((D, D), lambda i: (0, 0)),
            pl.BlockSpec((2, CHAINS, 16 // steps, 3, 16, 128), lambda i: (0, 0, i, 0, 0, 0)),
        ],
        out_specs=(
            pl.BlockSpec((SLOTS // steps, D), lambda i: (i, 0)),
            pl.BlockSpec((D // steps, D), lambda i: (i, 0)),
            pl.BlockSpec((D // steps, 256), lambda i: (i, 0)),
        ),
        compiler_params=pltpu.CompilerParams(vmem_limit_bytes=60 * 2**20),
    )(resid, rotation, tiles)
    return encoded, book.reshape(M, 8, 256), gram


def solution(mesh):
    return jax.shard_map(
        shards,
        mesh=mesh,
        in_specs=(
            P(("grp", "own"), None),
            P(("grp", "own")),
            P(("grp", "own"), None),
            P(),
            P("own", None),
            P(),
            P(),
        ),
        out_specs=(P(("grp", "own"), None), P(), P()),
        check_vma=False,
    )
```

time: 101 us -> 87.1 us (0.86)
  local copies, waits for them, and re-layouts: 6.86 us -> 0 us
  Pallas kernels: 93.1 us -> 86.3 us
    pallas_call x1, Pallas kernels: 93.1 us -> 80.6 us  [shards(): pl.pallas_call(kernel, out_shape=(jax.ShapeDtypeStruct((SLOTS, D), BF16),...]
    unnamed x8 -> x0, local copies, waits for them, and re-layouts: 6.86 us -> none
    pallas_call x0 -> x1, Pallas kernels: none -> 5.7 us  [shards(): pl.pallas_call(finish, grid=(steps,), out_shape=(jax.ShapeDtypeStruct((SL...]
where the time goes in v2:
time: 87.1 us; the launch traced here: 87 us
  Pallas kernels  86.3 us (99%)
    pallas_call x1, Pallas kernels, shards(): pl.pallas_call(kernel, out_shape=(jax.ShapeDtypeStruct((SLOTS, D), BF16),...  80.6 us
    pallas_call x1, Pallas kernels, shards(): pl.pallas_call(finish, grid=(steps,), out_shape=(jax.ShapeDtypeStruct((SL...  5.7 us

profile of v2, /device:TPU:1, one launch (start us, length us, event | category | flops | bytes accessed | tf_op | source)
XLA Modules:
  0.0 87.0 jit_solution(11751101280114516743)
XLA Ops:
  0.6 80.6 %shard_map.94 = (bf16[1024,768]{1,0:T(8,128)(2,1)}, bf16[2,4,16,3,16,128]{5,4,3,2,1,0:T(8,128)(2,1)}) custom-call(bf16[512,768]{1,0:T(8,128)(2,1)} %points_h.1, s32[1,512]{1,0:T(1,128)} %bitcast.6, s32[96,512]{1,0:T(8,128)} %bitcast.5, s32[512,128]{1,0:T(8,128)} %bitcast.4, bf16[512,768]{1,0:T(8,128)(2,1)} %centroids_h.1, bf16[768,768]{1,0:T(8,128)(2,1)} %rotation.1, ...), custom_call_target="tpu_custom_call" | custom-call | tf_op jit(solution)/shard_map/pallas_call | solution.py:519
  81.3 5.7 %shard_map.95 = (bf16[1024,768]{1,0:T(8,128)(2,1)}, f32[768,768]{1,0:T(8,128)}, f32[768,256]{1,0:T(8,128)}) custom-call(bf16[1024,768]{1,0:T(8,128)(2,1)} %get-tuple-element.8.resid, bf16[768,768]{1,0:T(8,128)(2,1)} %rotation.1, bf16[2,4,16,3,16,128]{5,4,3,2,1,0:T(8,128)(2,1)} %get-tuple-element.9.tiles), custom_call_target="tpu_custom_call" | custom-call | tf_op jit(solution)/shard_map/pallas_call | solution.py:539
